TPU v7x, 32 devices: a whole 2x2x4 slice. The times are simulated.
32 devices in a mesh: lon: 8 (over z, y), bin: 4 (over x, core).
Axes of the slice: x: 2, y: 2, z: 4, core: 2. Of those that a mesh axis runs over, the one named last changes fastest.
Arguments:
- adjoint_start: float32 [8, 4, 8, 1024], P('bin', None, None, 'lon'), may hold values from -6 to 6
- base_flux: float32 [8, 8, 1024], P('bin', None, 'lon'), may hold values from 0.1 to 1
- vertical_mixing: float32 [3, 8, 1024], P(None, None, 'lon'), may hold values from 0.05 to 5
- zonal_fraction: float32 [4, 8], replicated, may hold values from 0.02 to 0.98
- meridional_fraction: float32 [4], replicated, may hold values from 0.05 to 0.95
- zonal_hops: int32 [8], replicated, may hold values from -3 to 3, as said below
- cell_shift: int32 [8], replicated, may hold values from 0 to 127, as said below
Outputs:
- adjoint_end: float32 [8, 4, 8, 1024], P('bin', None, None, 'lon')
- emission_gradient: float32 [8, 1024], P(None, 'lon')
Inputs may be any that keep to these rules, and one draw needn't show every extreme that they name: For every h from 1 to 3, exactly (3 - h + 1) * 1 rows have zonal_hops >= h and exactly as many have zonal_hops <= -h. `cell_shift`: both extreme values occur.
All inputs are finite; a program needn't handle non-finite values.
Results may differ from a plain program's by a relative error of at most 0.0001.
Values sent between devices are 32-bit elements; how exact they have to be, the bound alone decides.
A program may use at most 64 MiB of HBM per device.

v0:
```python
import jax
import jax.numpy as jnp
from jax import lax
from jax.sharding import PartitionSpec as P

HMAX = 3
STEPS = 2


right_face = (0.0, -1.0, 7.0, 7.0, -1.0)
slope_face = (1.0, -8.0, 0.0, 8.0, -1.0)
curve_face = (3.0, -18.0, 30.0, -18.0, 3.0)


def padded_2(block, sides, width):
    for axis, dim in sides:
        count = lax.axis_size(axis)
        forward = [(i, i + 1) for i in range(count - 1)]
        forward.append((count - 1, 0))
        backward = [(target, source) for source, target in forward]
        low = lax.ppermute(
            lax.slice_in_dim(block, block.shape[dim] - width, None, axis=dim), axis, forward
        )
        high = lax.ppermute(lax.slice_in_dim(block, 0, width, axis=dim), axis, backward)
        block = jnp.concatenate([low, block, high], axis=dim)
    return block


def from_behind(value, axis, by):
    length = lax.axis_size(axis)
    return lax.ppermute(value, axis, [(i, (i + by) % length) for i in range(length)])


def flux_weights(courant):
    square = courant * courant
    cubic_part = 0.5 * square * (1.0 - courant * (2.0 / 3.0))
    return [
        (
            courant * right_face[offset]
            - 0.5 * square * slope_face[offset]
            + cubic_part * curve_face[offset]
        )
        / 12.0
        for offset in range(5)
    ]


def vertical_solve(adjoint_field, vertical_mixing):
    levels = adjoint_field.shape[1]
    ratios = []
    values = []
    for layer_index in range(levels):
        pivot_value = 1.0
        source_row = adjoint_field[:, layer_index]
        if layer_index < levels - 1:
            pivot_value = pivot_value + vertical_mixing[layer_index]
        if layer_index > 0:
            below = vertical_mixing[layer_index - 1]
            pivot_value = pivot_value + below + below * ratios[-1]
            source_row = source_row + below * values[-1]
        values.append(source_row / pivot_value)
        if layer_index < levels - 1:
            ratios.append(-vertical_mixing[layer_index] / pivot_value)
    solved = [values[levels - 1]]
    for layer_index in range(levels - 2, -1, -1):
        solved.insert(0, values[layer_index] - ratios[layer_index] * solved[0])
    return jnp.stack(solved, axis=1)


def zonal_adjoint(adjoint_field, zonal_fraction):
    sector_width = adjoint_field.shape[3]
    weights = flux_weights(zonal_fraction)
    padded = padded_2(adjoint_field, (("lon", 3),), 3)
    face_flux = 0.0
    for offset in range(5):
        start_col = 3 - (offset - 2)
        face_flux = (
            face_flux
            + weights[offset][:, :, None]
            * padded[:, :, :, start_col : start_col + sector_width + 1]
        )
    return adjoint_field - face_flux[:, :, :, :sector_width] + face_flux[:, :, :, 1:]


def roll_rows(field_data, offsets):
    width = field_data.shape[3]
    bit_count = max(1, (width - 1).bit_length())
    for bit_index in range(bit_count):
        amount = 1 << bit_index
        moved = jnp.roll(field_data, -amount, axis=3)
        chosen = (offsets // amount % 2)[None, None, :, None] == 1
        field_data = jnp.where(chosen, moved, field_data)
    return field_data


def pick_cells(adjoint_field, following, cell_shift):
    sector_width = adjoint_field.shape[3]
    joined = jnp.concatenate([adjoint_field, following], axis=3)
    return roll_rows(joined, cell_shift)[:, :, :, :sector_width]


def hop_shift(adjoint_field, zonal_hops, cell_shift):
    following = from_behind(adjoint_field, "lon", -1)
    picked = pick_cells(adjoint_field, following, cell_shift)
    hop_rows = zonal_hops[None, None, :, None]
    eastern = jnp.where(hop_rows > 0, picked, 0.0)
    western = jnp.where(hop_rows < 0, picked, 0.0)
    result_field = jnp.where(hop_rows == 0, picked, 0.0)
    for hop_count in range(1, HMAX + 1):
        eastern = from_behind(eastern, "lon", -1)
        western = from_behind(western, "lon", 1)
        result_field = result_field + jnp.where(hop_rows == hop_count, eastern, 0.0)
        result_field = result_field + jnp.where(hop_rows == -hop_count, western, 0.0)
    return result_field


def meridional_adjoint(adjoint_field, meridional_fraction):
    lat_count = adjoint_field.shape[2]
    weights = flux_weights(meridional_fraction)
    padded = jnp.pad(adjoint_field, ((0, 0), (0, 0), (3, 3), (0, 0)))
    face_flux = 0.0
    for offset in range(5):
        start_row = 3 - (offset - 2)
        face_flux = (
            face_flux
            + weights[offset][:, None, None] * padded[:, :, start_row : start_row + lat_count + 1]
        )
    return adjoint_field - face_flux[:, :, :lat_count] + face_flux[:, :, 1:]


def per_device(
    adjoint_start,
    base_flux,
    vertical_mixing,
    zonal_fraction,
    meridional_fraction,
    zonal_hops,
    cell_shift,
):
    adjoint_field = adjoint_start
    gradient_sum = jnp.zeros(base_flux.shape[1:], jnp.float32)
    for step_index in range(STEPS):
        adjoint_field = vertical_solve(adjoint_field, vertical_mixing)
        adjoint_field = zonal_adjoint(adjoint_field, zonal_fraction)
        adjoint_field = hop_shift(adjoint_field, zonal_hops, cell_shift)
        adjoint_field = meridional_adjoint(adjoint_field, meridional_fraction)
        local_term = jnp.sum(base_flux * adjoint_field[:, 0], axis=0)
        gradient_sum = gradient_sum + lax.psum(local_term, "bin")
    return (adjoint_field, gradient_sum)


def solution(mesh):
    return jax.shard_map(
        per_device,
        mesh=mesh,
        in_specs=(
            P("bin", None, None, "lon"),
            P("bin", None, "lon"),
            P(None, None, "lon"),
            P(),
            P(),
            P(),
            P(),
        ),
        out_specs=(P("bin", None, None, "lon"), P(None, "lon")),
        check_vma=False,
    )
```

profile of v0, /device:TPU:0, one launch (start us, length us, event | category | flops | bytes accessed | tf_op | source)
XLA Modules:
  0.0 83.2 jit_solution(6797585602489341325)
XLA Ops:
  0.6 0.8 fusion.54
  1.4 0.7 copy-done.2
  2.3 6.0 %collective-permute-start = (f32[2,4,8,3]{3,2,1,0:T(8,128)S(1)}, f32[2,4,8,3]{3,2,1,0:T(8,128)S(1)}, u32[]{:S(2)}, u32[]{:S(2)}) collective-permute-start(f32[2,4,8,3]{3,2,1,0:T(8,128)S(1)} %get-tuple-element.30), channel_id=1, source_target_pairs={{4,0},{8,4},{12,8},{16,12},{20,16},{24,20},{28,24},{0,28},{5,1},{9... | collective-permute-start | bytes 2312 | tf_op jit(solution)/shard_map/ppermute | solution.py:24
  8.3 0.6 copy-done.5
  9.0 0.9 %collective-permute-done = f32[2,4,8,3]{3,2,1,0:T(8,128)S(1)} collective-permute-done((f32[2,4,8,3]{3,2,1,0:T(8,128)S(1)}, f32[2,4,8,3]{3,2,1,0:T(8,128)S(1)}, u32[]{:S(2)}, u32[]{:S(2)}) %collective-permute-start) | collective-permute-done | bytes 800 | tf_op jit(solution)/shard_map/ppermute | solution.py:24
  9.9 5.0 %collective-permute-done.1 = f32[2,4,8,3]{3,2,1,0:T(8,128)S(1)} collective-permute-done((f32[2,4,8,3]{3,2,1,0:T(8,128)S(1)}, f32[2,4,8,3]{3,2,1,0:T(8,128)S(1)}, u32[]{:S(2)}, u32[]{:S(2)}) %collective-permute-start.1) | collective-permute-done | bytes 800 | tf_op jit(solution)/shard_map/ppermute | solution.py:21
  14.9 0.1 pad_maximum_fusion.2
  15.0 0.2 fusion.26
  15.2 0.1 slice_add_fusion.3
  15.3 0.6 copy-done.6
  15.9 3.3 %collective-permute-done.2 = f32[2,4,8,128]{3,2,1,0:T(8,128)S(1)} collective-permute-done((f32[2,4,8,128]{3,2,1,0:T(8,128)S(1)}, f32[2,4,8,128]{3,2,1,0:T(8,128)S(1)}, u32[]{:S(2)}, u32[]{:S(2)}) %collective-permute-start.2) | collective-permute-done | bytes 32800 | tf_op jit(solution)/shard_map/ppermute | solution.py:31
  19.2 0.1 fusion.2
  19.3 0.1 fusion.3
  19.4 0.1 slice.368
  19.5 0.1 maximum_select_fusion
  19.5 0.1 slice.370
  19.6 0.1 maximum_select_fusion.1
  19.7 0.1 slice.372
  19.8 0.1 maximum_select_fusion.2
  19.9 0.1 slice.374
  20.0 0.1 maximum_select_fusion.3
  20.1 0.1 slice.376
  20.2 0.1 maximum_select_fusion.4
  20.3 0.1 slice.378
  20.4 0.1 maximum_select_fusion.5
  20.5 0.1 broadcast_select_fusion.2
  20.6 4.7 %collective-permute-start.3 = (f32[2,4,8,128]{3,2,1,0:T(8,128)S(1)}, f32[2,4,8,128]{3,2,1,0:T(8,128)S(1)}, u32[]{:S(2)}, u32[]{:S(2)}) collective-permute-start(f32[2,4,8,128]{3,2,1,0:T(8,128)S(1)} %get-tuple-element.10), channel_id=1, source_target_pairs={{0,28},{4,0},{8,4},{12,8},{16,12},{20,16},{24,20},{28,24},{1,29},{... | collective-permute-start | bytes 98312 | tf_op jit(solution)/shard_map/ppermute | solution.py:31
  25.4 1.9 %collective-permute-done.4 = f32[2,4,8,128]{3,2,1,0:T(8,128)S(1)} collective-permute-done((f32[2,4,8,128]{3,2,1,0:T(8,128)S(1)}, f32[2,4,8,128]{3,2,1,0:T(8,128)S(1)}, u32[]{:S(2)}, u32[]{:S(2)}) %collective-permute-start.4) | collective-permute-done | bytes 32800 | tf_op jit(solution)/shard_map/ppermute | solution.py:31
  27.2 4.8 %collective-permute-start.5 = (f32[2,4,8,128]{3,2,1,0:T(8,128)S(1)}, f32[2,4,8,128]{3,2,1,0:T(8,128)S(1)}, u32[]{:S(2)}, u32[]{:S(2)}) collective-permute-start(f32[2,4,8,128]{3,2,1,0:T(8,128)S(1)} %collective-permute-done.3), channel_id=1, source_target_pairs={{0,28},{4,0},{8,4},{12,8},{16,12},{20,16},{24,20},{28,24},{1,29},{... | collective-permute-start | bytes 98312 | tf_op jit(solution)/shard_map/ppermute | solution.py:31
  32.1 1.8 %collective-permute-done.6 = f32[2,4,8,128]{3,2,1,0:T(8,128)S(1)} collective-permute-done((f32[2,4,8,128]{3,2,1,0:T(8,128)S(1)}, f32[2,4,8,128]{3,2,1,0:T(8,128)S(1)}, u32[]{:S(2)}, u32[]{:S(2)}) %collective-permute-start.6) | collective-permute-done | bytes 32800 | tf_op jit(solution)/shard_map/ppermute | solution.py:31
  33.9 5.0 %collective-permute-start.7 = (f32[2,4,8,128]{3,2,1,0:T(8,128)S(1)}, f32[2,4,8,128]{3,2,1,0:T(8,128)S(1)}, u32[]{:S(2)}, u32[]{:S(2)}) collective-permute-start(f32[2,4,8,128]{3,2,1,0:T(8,128)S(1)} %collective-permute-done.5), channel_id=1, source_target_pairs={{0,28},{4,0},{8,4},{12,8},{16,12},{20,16},{24,20},{28,24},{1,29},{... | collective-permute-start | bytes 98312 | tf_op jit(solution)/shard_map/ppermute | solution.py:31
  38.8 2.0 %collective-permute-done.8 = f32[2,4,8,128]{3,2,1,0:T(8,128)S(1)} collective-permute-done((f32[2,4,8,128]{3,2,1,0:T(8,128)S(1)}, f32[2,4,8,128]{3,2,1,0:T(8,128)S(1)}, u32[]{:S(2)}, u32[]{:S(2)}) %collective-permute-start.8) | collective-permute-done | bytes 32800 | tf_op jit(solution)/shard_map/ppermute | solution.py:31
  40.8 0.1 select_add_fusion.1
  40.9 0.1 fusion.8
  41.1 4.7 %collective-permute-start.9 = (f32[2,4,8,3]{3,2,1,0:T(8,128)S(1)}, f32[2,4,8,3]{3,2,1,0:T(8,128)S(1)}, u32[]{:S(2)}, u32[]{:S(2)}) collective-permute-start(f32[2,4,8,3]{3,2,1,0:T(8,128)S(1)} %get-tuple-element.26), channel_id=1, source_target_pairs={{4,0},{8,4},{12,8},{16,12},{20,16},{24,20},{28,24},{0,28},{5,1},{9... | collective-permute-start | bytes 2312 | tf_op jit(solution)/shard_map/ppermute | solution.py:24
  45.9 1.9 %collective-permute-done.10 = f32[2,4,8,3]{3,2,1,0:T(8,128)S(1)} collective-permute-done((f32[2,4,8,3]{3,2,1,0:T(8,128)S(1)}, f32[2,4,8,3]{3,2,1,0:T(8,128)S(1)}, u32[]{:S(2)}, u32[]{:S(2)}) %collective-permute-start.10) | collective-permute-done | bytes 800 | tf_op jit(solution)/shard_map/ppermute | solution.py:21
  47.8 0.1 pad_maximum_fusion.3
  47.8 0.2 fusion.22
  48.0 0.1 slice_add_fusion.1
  48.1 4.7 %collective-permute-start.11 = (f32[2,4,8,128]{3,2,1,0:T(8,128)S(1)}, f32[2,4,8,128]{3,2,1,0:T(8,128)S(1)}, u32[]{:S(2)}, u32[]{:S(2)}) collective-permute-start(f32[2,4,8,128]{3,2,1,0:T(8,128)S(1)} %slice_add_fusion.1), channel_id=1, source_target_pairs={{0,28},{4,0},{8,4},{12,8},{16,12},{20,16},{24,20},{28,24},{1,29},{... | collective-permute-start | bytes 98312 | tf_op jit(solution)/shard_map/ppermute | solution.py:31
  52.8 1.6 %collective-permute-done.11 = f32[2,4,8,128]{3,2,1,0:T(8,128)S(1)} collective-permute-done((f32[2,4,8,128]{3,2,1,0:T(8,128)S(1)}, f32[2,4,8,128]{3,2,1,0:T(8,128)S(1)}, u32[]{:S(2)}, u32[]{:S(2)}) %collective-permute-start.11) | collective-permute-done | bytes 32800 | tf_op jit(solution)/shard_map/ppermute | solution.py:31
  54.4 0.1 fusion
  54.5 0.1 fusion.1
  54.6 0.1 slice.401
  54.7 0.1 maximum_select_fusion.6
  54.8 0.1 slice.403
  54.9 0.1 maximum_select_fusion.7
  55.0 0.1 slice.405
  55.0 0.1 maximum_select_fusion.8
  55.1 0.1 slice.407
  55.2 0.1 maximum_select_fusion.9
  55.4 0.1 maximum_select_fusion.10
  55.6 0.1 maximum_select_fusion.11
  55.7 0.1 broadcast_select_fusion.3
  55.9 5.1 %collective-permute-start.12 = (f32[2,4,8,128]{3,2,1,0:T(8,128)S(1)}, f32[2,4,8,128]{3,2,1,0:T(8,128)S(1)}, u32[]{:S(2)}, u32[]{:S(2)}) collective-permute-start(f32[2,4,8,128]{3,2,1,0:T(8,128)S(1)} %get-tuple-element.4), channel_id=1, source_target_pairs={{0,28},{4,0},{8,4},{12,8},{16,12},{20,16},{24,20},{28,24},{1,29},{... | collective-permute-start | bytes 98312 | tf_op jit(solution)/shard_map/ppermute | solution.py:31
  60.9 1.8 %collective-permute-done.13 = f32[2,4,8,128]{3,2,1,0:T(8,128)S(1)} collective-permute-done((f32[2,4,8,128]{3,2,1,0:T(8,128)S(1)}, f32[2,4,8,128]{3,2,1,0:T(8,128)S(1)}, u32[]{:S(2)}, u32[]{:S(2)}) %collective-permute-start.13) | collective-permute-done | bytes 32800 | tf_op jit(solution)/shard_map/ppermute | solution.py:31
  62.8 4.8 %collective-permute-start.14 = (f32[2,4,8,128]{3,2,1,0:T(8,128)S(1)}, f32[2,4,8,128]{3,2,1,0:T(8,128)S(1)}, u32[]{:S(2)}, u32[]{:S(2)}) collective-permute-start(f32[2,4,8,128]{3,2,1,0:T(8,128)S(1)} %collective-permute-done.12), channel_id=1, source_target_pairs={{0,28},{4,0},{8,4},{12,8},{16,12},{20,16},{24,20},{28,24},{1,29},{... | collective-permute-start | bytes 98312 | tf_op jit(solution)/shard_map/ppermute | solution.py:31
  67.5 1.8 %collective-permute-done.15 = f32[2,4,8,128]{3,2,1,0:T(8,128)S(1)} collective-permute-done((f32[2,4,8,128]{3,2,1,0:T(8,128)S(1)}, f32[2,4,8,128]{3,2,1,0:T(8,128)S(1)}, u32[]{:S(2)}, u32[]{:S(2)}) %collective-permute-start.15) | collective-permute-done | bytes 32800 | tf_op jit(solution)/shard_map/ppermute | solution.py:31
  69.4 4.8 %collective-permute-start.16 = (f32[2,4,8,128]{3,2,1,0:T(8,128)S(1)}, f32[2,4,8,128]{3,2,1,0:T(8,128)S(1)}, u32[]{:S(2)}, u32[]{:S(2)}) collective-permute-start(f32[2,4,8,128]{3,2,1,0:T(8,128)S(1)} %collective-permute-done.14), channel_id=1, source_target_pairs={{0,28},{4,0},{8,4},{12,8},{16,12},{20,16},{24,20},{28,24},{1,29},{... | collective-permute-start | bytes 98312 | tf_op jit(solution)/shard_map/ppermute | solution.py:31
  74.2 1.8 %collective-permute-done.17 = f32[2,4,8,128]{3,2,1,0:T(8,128)S(1)} collective-permute-done((f32[2,4,8,128]{3,2,1,0:T(8,128)S(1)}, f32[2,4,8,128]{3,2,1,0:T(8,128)S(1)}, u32[]{:S(2)}, u32[]{:S(2)}) %collective-permute-start.17) | collective-permute-done | bytes 32800 | tf_op jit(solution)/shard_map/ppermute | solution.py:31
  76.0 0.1 select_add_fusion
  76.1 0.1 fusion.17
  76.2 0.7 copy-done.3
  76.9 6.3 %psum.16 = f32[8,128]{1,0:T(8,128)} all-reduce(f32[8,128]{1,0:T(8,128)S(1)} %add.377), channel_id=1, replica_groups=mesh['lon'=8,'bin'=4] {'bin'}, use_global_device_ids=true, to_apply=%region_1.2 | all-reduce | flops 1024 | bytes 8192 | tf_op jit(solution)/shard_map/psum | solution.py:148
  (64 shorter events, 0.8 us)
Async XLA Ops:
  0.6 0.8 copy-start
  1.4 0.8 copy-start.2
  2.3 6.0 %copy-start.4 = (f32[4,8]{1,0:T(4,128)S(1)}, f32[4,8]{1,0:T(4,128)}, u32[]{:S(2)}) copy-start(f32[4,8]{1,0:T(4,128)} %param.10) | copy-start | bytes 388
  2.3 7.6 %collective-permute-start = (f32[2,4,8,3]{3,2,1,0:T(8,128)S(1)}, f32[2,4,8,3]{3,2,1,0:T(8,128)S(1)}, u32[]{:S(2)}, u32[]{:S(2)}) collective-permute-start(f32[2,4,8,3]{3,2,1,0:T(8,128)S(1)} %get-tuple-element.30), channel_id=1, source_target_pairs={{4,0},{8,4},{12,8},{16,12},{20,16},{24,20},{28,24},{0,28},{5,1},{9... | collective-permute-start | bytes 2312 | tf_op jit(solution)/shard_map/ppermute | solution.py:24
  8.3 0.7 copy-start.5
  8.3 6.6 %collective-permute-start.1 = (f32[2,4,8,3]{3,2,1,0:T(8,128)S(1)}, f32[2,4,8,3]{3,2,1,0:T(8,128)S(1)}, u32[]{:S(2)}, u32[]{:S(2)}) collective-permute-start(f32[2,4,8,3]{3,2,1,0:T(8,128)S(1)} %get-tuple-element.31), channel_id=1, source_target_pairs={{0,4},{4,8},{8,12},{12,16},{16,20},{20,24},{24,28},{28,0},{1,5},{5... | collective-permute-start | bytes 2312 | tf_op jit(solution)/shard_map/ppermute | solution.py:21
  15.2 0.7 copy-start.6
  15.3 3.9 %collective-permute-start.2 = (f32[2,4,8,128]{3,2,1,0:T(8,128)S(1)}, f32[2,4,8,128]{3,2,1,0:T(8,128)S(1)}, u32[]{:S(2)}, u32[]{:S(2)}) collective-permute-start(f32[2,4,8,128]{3,2,1,0:T(8,128)S(1)} %slice_add_fusion.3), channel_id=1, source_target_pairs={{0,28},{4,0},{8,4},{12,8},{16,12},{20,16},{24,20},{28,24},{1,29},{... | collective-permute-start | bytes 98312 | tf_op jit(solution)/shard_map/ppermute | solution.py:31
  20.6 18.2 %copy-start.7 = (f32[4]{0:T(128)S(1)}, f32[4]{0:T(128)}, u32[]{:S(2)}) copy-start(f32[4]{0:T(128)} %param.11) | copy-start | bytes 52
  20.6 6.6 %collective-permute-start.4 = (f32[2,4,8,128]{3,2,1,0:T(8,128)S(1)}, f32[2,4,8,128]{3,2,1,0:T(8,128)S(1)}, u32[]{:S(2)}, u32[]{:S(2)}) collective-permute-start(f32[2,4,8,128]{3,2,1,0:T(8,128)S(1)} %broadcast_select_fusion.1), channel_id=1, source_target_pairs={{0,4},{4,8},{8,12},{12,16},{16,20},{20,24},{24,28},{28,0},{1,5},{5... | collective-permute-start | bytes 98312 | tf_op jit(solution)/shard_map/ppermute | solution.py:31
  20.6 6.6 %collective-permute-start.3 = (f32[2,4,8,128]{3,2,1,0:T(8,128)S(1)}, f32[2,4,8,128]{3,2,1,0:T(8,128)S(1)}, u32[]{:S(2)}, u32[]{:S(2)}) collective-permute-start(f32[2,4,8,128]{3,2,1,0:T(8,128)S(1)} %get-tuple-element.10), channel_id=1, source_target_pairs={{0,28},{4,0},{8,4},{12,8},{16,12},{20,16},{24,20},{28,24},{1,29},{... | collective-permute-start | bytes 98312 | tf_op jit(solution)/shard_map/ppermute | solution.py:31
  27.2 6.6 %collective-permute-start.6 = (f32[2,4,8,128]{3,2,1,0:T(8,128)S(1)}, f32[2,4,8,128]{3,2,1,0:T(8,128)S(1)}, u32[]{:S(2)}, u32[]{:S(2)}) collective-permute-start(f32[2,4,8,128]{3,2,1,0:T(8,128)S(1)} %collective-permute-done.4), channel_id=1, source_target_pairs={{0,4},{4,8},{8,12},{12,16},{16,20},{20,24},{24,28},{28,0},{1,5},{5... | collective-permute-start | bytes 98312 | tf_op jit(solution)/shard_map/ppermute | solution.py:31
  27.2 6.6 %collective-permute-start.5 = (f32[2,4,8,128]{3,2,1,0:T(8,128)S(1)}, f32[2,4,8,128]{3,2,1,0:T(8,128)S(1)}, u32[]{:S(2)}, u32[]{:S(2)}) collective-permute-start(f32[2,4,8,128]{3,2,1,0:T(8,128)S(1)} %collective-permute-done.3), channel_id=1, source_target_pairs={{0,28},{4,0},{8,4},{12,8},{16,12},{20,16},{24,20},{28,24},{1,29},{... | collective-permute-start | bytes 98312 | tf_op jit(solution)/shard_map/ppermute | solution.py:31
  33.9 6.9 %collective-permute-start.8 = (f32[2,4,8,128]{3,2,1,0:T(8,128)S(1)}, f32[2,4,8,128]{3,2,1,0:T(8,128)S(1)}, u32[]{:S(2)}, u32[]{:S(2)}) collective-permute-start(f32[2,4,8,128]{3,2,1,0:T(8,128)S(1)} %collective-permute-done.6), channel_id=1, source_target_pairs={{0,4},{4,8},{8,12},{12,16},{16,20},{20,24},{24,28},{28,0},{1,5},{5... | collective-permute-start | bytes 98312 | tf_op jit(solution)/shard_map/ppermute | solution.py:31
  33.9 6.9 %collective-permute-start.7 = (f32[2,4,8,128]{3,2,1,0:T(8,128)S(1)}, f32[2,4,8,128]{3,2,1,0:T(8,128)S(1)}, u32[]{:S(2)}, u32[]{:S(2)}) collective-permute-start(f32[2,4,8,128]{3,2,1,0:T(8,128)S(1)} %collective-permute-done.5), channel_id=1, source_target_pairs={{0,28},{4,0},{8,4},{12,8},{16,12},{20,16},{24,20},{28,24},{1,29},{... | collective-permute-start | bytes 98312 | tf_op jit(solution)/shard_map/ppermute | solution.py:31
  41.1 6.6 %collective-permute-start.10 = (f32[2,4,8,3]{3,2,1,0:T(8,128)S(1)}, f32[2,4,8,3]{3,2,1,0:T(8,128)S(1)}, u32[]{:S(2)}, u32[]{:S(2)}) collective-permute-start(f32[2,4,8,3]{3,2,1,0:T(8,128)S(1)} %get-tuple-element.27), channel_id=1, source_target_pairs={{0,4},{4,8},{8,12},{12,16},{16,20},{20,24},{24,28},{28,0},{1,5},{5... | collective-permute-start | bytes 2312 | tf_op jit(solution)/shard_map/ppermute | solution.py:21
  41.1 6.6 %collective-permute-start.9 = (f32[2,4,8,3]{3,2,1,0:T(8,128)S(1)}, f32[2,4,8,3]{3,2,1,0:T(8,128)S(1)}, u32[]{:S(2)}, u32[]{:S(2)}) collective-permute-start(f32[2,4,8,3]{3,2,1,0:T(8,128)S(1)} %get-tuple-element.26), channel_id=1, source_target_pairs={{4,0},{8,4},{12,8},{16,12},{20,16},{24,20},{28,24},{0,28},{5,1},{9... | collective-permute-start | bytes 2312 | tf_op jit(solution)/shard_map/ppermute | solution.py:24
  48.1 6.3 %collective-permute-start.11 = (f32[2,4,8,128]{3,2,1,0:T(8,128)S(1)}, f32[2,4,8,128]{3,2,1,0:T(8,128)S(1)}, u32[]{:S(2)}, u32[]{:S(2)}) collective-permute-start(f32[2,4,8,128]{3,2,1,0:T(8,128)S(1)} %slice_add_fusion.1), channel_id=1, source_target_pairs={{0,28},{4,0},{8,4},{12,8},{16,12},{20,16},{24,20},{28,24},{1,29},{... | collective-permute-start | bytes 98312 | tf_op jit(solution)/shard_map/ppermute | solution.py:31
  55.9 6.9 %collective-permute-start.13 = (f32[2,4,8,128]{3,2,1,0:T(8,128)S(1)}, f32[2,4,8,128]{3,2,1,0:T(8,128)S(1)}, u32[]{:S(2)}, u32[]{:S(2)}) collective-permute-start(f32[2,4,8,128]{3,2,1,0:T(8,128)S(1)} %broadcast_select_fusion), channel_id=1, source_target_pairs={{0,4},{4,8},{8,12},{12,16},{16,20},{20,24},{24,28},{28,0},{1,5},{5... | collective-permute-start | bytes 98312 | tf_op jit(solution)/shard_map/ppermute | solution.py:31
  55.9 6.9 %collective-permute-start.12 = (f32[2,4,8,128]{3,2,1,0:T(8,128)S(1)}, f32[2,4,8,128]{3,2,1,0:T(8,128)S(1)}, u32[]{:S(2)}, u32[]{:S(2)}) collective-permute-start(f32[2,4,8,128]{3,2,1,0:T(8,128)S(1)} %get-tuple-element.4), channel_id=1, source_target_pairs={{0,28},{4,0},{8,4},{12,8},{16,12},{20,16},{24,20},{28,24},{1,29},{... | collective-permute-start | bytes 98312 | tf_op jit(solution)/shard_map/ppermute | solution.py:31
  62.8 6.6 %collective-permute-start.15 = (f32[2,4,8,128]{3,2,1,0:T(8,128)S(1)}, f32[2,4,8,128]{3,2,1,0:T(8,128)S(1)}, u32[]{:S(2)}, u32[]{:S(2)}) collective-permute-start(f32[2,4,8,128]{3,2,1,0:T(8,128)S(1)} %collective-permute-done.13), channel_id=1, source_target_pairs={{0,4},{4,8},{8,12},{12,16},{16,20},{20,24},{24,28},{28,0},{1,5},{5... | collective-permute-start | bytes 98312 | tf_op jit(solution)/shard_map/ppermute | solution.py:31
  62.8 6.6 %collective-permute-start.14 = (f32[2,4,8,128]{3,2,1,0:T(8,128)S(1)}, f32[2,4,8,128]{3,2,1,0:T(8,128)S(1)}, u32[]{:S(2)}, u32[]{:S(2)}) collective-permute-start(f32[2,4,8,128]{3,2,1,0:T(8,128)S(1)} %collective-permute-done.12), channel_id=1, source_target_pairs={{0,28},{4,0},{8,4},{12,8},{16,12},{20,16},{24,20},{28,24},{1,29},{... | collective-permute-start | bytes 98312 | tf_op jit(solution)/shard_map/ppermute | solution.py:31
  69.4 6.6 %collective-permute-start.17 = (f32[2,4,8,128]{3,2,1,0:T(8,128)S(1)}, f32[2,4,8,128]{3,2,1,0:T(8,128)S(1)}, u32[]{:S(2)}, u32[]{:S(2)}) collective-permute-start(f32[2,4,8,128]{3,2,1,0:T(8,128)S(1)} %collective-permute-done.15), channel_id=1, source_target_pairs={{0,4},{4,8},{8,12},{12,16},{16,20},{20,24},{24,28},{28,0},{1,5},{5... | collective-permute-start | bytes 98312 | tf_op jit(solution)/shard_map/ppermute | solution.py:31
  69.4 6.6 %collective-permute-start.16 = (f32[2,4,8,128]{3,2,1,0:T(8,128)S(1)}, f32[2,4,8,128]{3,2,1,0:T(8,128)S(1)}, u32[]{:S(2)}, u32[]{:S(2)}) collective-permute-start(f32[2,4,8,128]{3,2,1,0:T(8,128)S(1)} %collective-permute-done.14), channel_id=1, source_target_pairs={{0,28},{4,0},{8,4},{12,8},{16,12},{20,16},{24,20},{28,24},{1,29},{... | collective-permute-start | bytes 98312 | tf_op jit(solution)/shard_map/ppermute | solution.py:31
  76.2 0.7 copy-start.3
  76.9 6.3 %copy-start.1 = (f32[2,4,8,128]{3,2,1,0:T(8,128)}, f32[2,4,8,128]{3,2,1,0:T(8,128)S(1)}, u32[]{:S(2)}) copy-start(f32[2,4,8,128]{3,2,1,0:T(8,128)S(1)} %slice_add_fusion) | copy-start | bytes 98308
where the time goes:
time: 83.5 us; the launch traced here: 83.2 us
  starting transfers between devices  44.6 us (53%)
  waiting for transfers between devices  23.9 us (29%)
  blocking collectives  6.26 us (7%)
  local copies, waits for them, and re-layouts  3.77 us (5%)
  other arithmetic  3.62 us (4%)
  between operations  1.04 us (1%)
    ppermute x14, starting transfers between devices, from_behind(): lax.ppermute(value, axis, [(i, (i + by) % length) for i in range(length)])  33.8 us
    ppermute x14, waiting for transfers between devices, from_behind(): lax.ppermute(value, axis, [(i, (i + by) % length) for i in range(length)])  16.1 us
    ppermute x2, starting transfers between devices, padded_2(): lax.ppermute(lax.slice_in_dim(block, 0, width, axis=dim), axis, backward)  10.7 us
    ppermute x2, waiting for transfers between devices, padded_2(): lax.ppermute(lax.slice_in_dim(block, block.shape[dim] - width, None, axis...  6.9 us
    psum x1, blocking collectives, per_device(): gradient_sum = gradient_sum + lax.psum(local_term, 'bin')  6.26 us
    unnamed x16, local copies, waits for them, and re-layouts  2.61 us
  transfers between devices with their start and end apart: 18, of which 11 were waited for; matrix products, arithmetic and copies ran while one was open for 0% of the time, Pallas kernels for 0%

commit v1 on v0

v1 whole, which is shorter than its diff:
```python
import functools

import jax
import jax.numpy as jnp
from jax import lax
from jax.experimental import pallas as pl
from jax.experimental.pallas import tpu as pltpu
from jax.sharding import PartitionSpec as P

HMAX = 3
STEPS = 2
MESH = pl.DeviceIdType.MESH

right_face = (0.0, -1.0, 7.0, 7.0, -1.0)
slope_face = (1.0, -8.0, 0.0, 8.0, -1.0)
curve_face = (3.0, -18.0, 30.0, -18.0, 3.0)


def flux_weights(courant):
    square = courant * courant
    cubic_part = 0.5 * square * (1.0 - courant * (2.0 / 3.0))
    return [
        (
            courant * right_face[offset]
            - 0.5 * square * slope_face[offset]
            + cubic_part * curve_face[offset]
        )
        * (1.0 / 12.0)
        for offset in range(5)
    ]


def taps(courant):
    a = flux_weights(courant)
    return [-a[4], a[4] - a[3], 1.0 + a[3] - a[2], a[2] - a[1], a[1] - a[0], a[0]]


def loop(count, body):
    if count <= 8:
        for i in range(count):
            body(i)
    else:

        @pl.loop(0, count)
        def _(i):
            body(i)


class Plan:
    def __init__(self, rows, unit, ring):
        self.ring = ring
        count = {h: unit for h in range(-HMAX, HMAX + 1)}
        count[0] = rows - 2 * HMAX * unit
        self.count = count
        self.start = {}
        at = 0
        for h in range(-HMAX, HMAX + 1):
            self.start[h] = at
            at += count[h]
        self.offsets = [t for t in range(-HMAX - 2, HMAX + 2) if t % ring]
        self.offsets.sort(key=lambda t: -abs(t))
        self.slot = {t: i for i, t in enumerate(self.offsets)}

    def span(self, t):
        low, high = max(-t - 2, -HMAX), min(-t + 1, HMAX)
        first = self.start[low]
        return first, self.start[high] + self.count[high] - first


def kernel(
    plan,
    nbin,
    adj_ref,
    flux_ref,
    mix_ref,
    zf_ref,
    mf_ref,
    hops_ref,
    cells_ref,
    end_ref,
    grad_ref,
    rank,
    shifts_of,
    natural_c,
    mixed,
    sends,
    recvs,
    wz,
    wm,
    zonal,
    padded,
    result,
    gbuf,
    send_sem,
    recv_sem,
    gsend_sem,
    grecv_sem,
):
    bins, levels, rows, width = adj_ref.shape
    bl = bins * levels
    ring = plan.ring
    lon, mybin = lax.axis_index("lon"), lax.axis_index("bin")

    barrier = pltpu.get_barrier_semaphore()
    shifts = sorted({t % ring for t in plan.offsets})
    for t in shifts:
        pl.semaphore_signal(
            barrier, inc=1, device_id=(lax.rem(lon + ring - t, ring), mybin), device_id_type=MESH
        )
    for o in range(1, nbin):
        pl.semaphore_signal(
            barrier, inc=1, device_id=(lon, lax.rem(mybin + nbin - o, nbin)), device_id_type=MESH
        )

    inverse, ratios, mix = [], [], [mix_ref[l] for l in range(levels - 1)]
    for l in range(levels):
        pivot = 1.0
        if l < levels - 1:
            pivot = pivot + mix[l]
        if l > 0:
            pivot = pivot + mix[l - 1] + mix[l - 1] * ratios[-1]
        inverse.append(1.0 / pivot)
        if l < levels - 1:
            ratios.append(-mix[l] * inverse[l])

    def at(row):
        if isinstance(row, int):
            return pl.ds(row * bl, bl)
        return pl.ds(pl.multiple_of(row * bl, bl), bl)

    def column(index):
        return pl.ds(index, rows, stride=bl)

    def vertical(field):
        for b in range(bins):
            values = []
            for l in range(levels):
                source = field(b, l)
                if l > 0:
                    source = source + mix[l - 1] * values[-1]
                values.append(source * inverse[l])
            solved = values[levels - 1]
            mixed[column(b * levels + levels - 1), :] = solved
            for l in range(levels - 2, -1, -1):
                solved = values[l] - ratios[l] * solved
                mixed[column(b * levels + l), :] = solved

    level_of = lax.rem(lax.broadcasted_iota(jnp.int32, (bl, width), 0), levels)
    lane = lax.broadcasted_iota(jnp.int32, (bl, width), 1)

    def by_level(value):
        out = jnp.full((bl, width), value(0), jnp.float32)
        for l in range(1, levels):
            out = jnp.where(level_of == l, value(l), out)
        return out

    def splat(value):
        return jnp.full((bl, width), value, jnp.int32)

    def fold(one, start):
        if rows <= 8:
            for i in range(rows):
                start = one(i, start)
            return start
        return lax.fori_loop(0, rows, one, start)

    def find_rank(j):
        mine = splat(hops_ref[j])

        def one(i, total):
            ahead = jnp.where(i < j, 1, 0) if rows > 8 else int(i < j)
            return total + jnp.where(splat(hops_ref[i]) < mine + ahead, 1, 0)

        rank[at(j), :] = fold(one, splat(0))

    def ordered(source, p):
        def one(j, value):
            return jnp.where(rank[at(j), :] == p, source(j), value)

        return fold(one, source(0))

    def copies(step):
        found = []
        for t in plan.offsets:
            first, count = plan.span(t)
            part = pl.ds(first * bl, count * bl)
            i = plan.slot[t]
            found.append(
                pltpu.make_async_remote_copy(
                    src_ref=sends.at[step, part],
                    dst_ref=recvs.at[step, i, part],
                    send_sem=send_sem.at[step, i],
                    recv_sem=recv_sem.at[step, i],
                    device_id=(lax.rem(lon + (t % ring), ring), mybin),
                    device_id_type=MESH,
                )
            )
        return found

    def natural(b, l):
        return result[column(b * levels + l), :]

    gradient = None
    for step in range(STEPS):
        vertical(natural if step else (lambda b, l: adj_ref[b, l]))

        def arrange(p):
            sends[step, at(p), :] = ordered(lambda j: mixed[at(j), :], p)

        if step == 0:
            loop(rows, find_rank)
        loop(rows, arrange)

        if step == 0:
            pl.semaphore_wait(barrier, len(shifts) + nbin - 1)
        moving = copies(step)
        for copy in moving:
            copy.start()

        if step == 0:

            def courant(j):
                natural_c[at(j), :] = by_level(lambda l: zf_ref[l, j])

            loop(rows, courant)

            def zonal_weights(p):
                fraction = ordered(lambda j: natural_c[at(j), :], p)
                for s, value in enumerate(taps(fraction)):
                    wz[s, at(p), :] = value
                shifts_of[at(p), :] = ordered(lambda j: splat(cells_ref[j]), p)

            loop(rows, zonal_weights)
            for s, value in enumerate(taps(by_level(lambda l: mf_ref[l]))):
                wm[s] = value
            nothing = jnp.zeros((bl, width), jnp.float32)
            for row in (0, 1, rows + 2, rows + 3, rows + 4):
                padded[at(row), :] = nothing
        else:
            gradient = sum(flux_ref[b] * natural(b, 0) for b in range(bins))

        for copy in moving:
            copy.wait_recv()

        for h in range(-HMAX, HMAX + 1):

            def shift(i):
                p = plan.start[h] + i

                def tile(k):
                    t = -h - k
                    if t % ring == 0:
                        return sends[step, at(p), :]
                    return recvs[step, plan.slot[t], at(p), :]

                cells = shifts_of[at(p), :]
                short = cells < 2
                first = cells - 2 + jnp.where(short, width, 0)
                t0, t1, t2, t3 = tile(-1), tile(0), tile(1), tile(2)
                ra = jnp.where(short, t0, t1)
                rb = jnp.where(short, t1, t2)
                rc = jnp.where(short, t2, t3)
                for bit in range((width - 1).bit_length()):
                    chosen = (first & (1 << bit)) != 0
                    turn = width - (1 << bit)
                    ra = jnp.where(chosen, pltpu.roll(ra, turn, 1), ra)
                    rb = jnp.where(chosen, pltpu.roll(rb, turn, 1), rb)
                    rc = jnp.where(chosen, pltpu.roll(rc, turn, 1), rc)
                inside = lane < width - first
                w0 = jnp.where(inside, ra, rb)
                w1 = jnp.where(inside, rb, rc)
                out = wz[0, at(p), :] * w0
                for s in range(1, 6):
                    moved = pltpu.roll(jnp.where(lane < s, w1, w0), width - s, 1)
                    out = out + wz[s, at(p), :] * moved
                zonal[at(p), :] = out

            loop(plan.count[h], shift)

        def back(j):
            place = rank[at(j), :]

            def one(p, value):
                return jnp.where(place == p, zonal[at(p), :], value)

            padded[at(j + 2), :] = fold(one, zonal[at(0), :])

        loop(rows, back)

        def meridional(j):
            out = wm[0] * padded[at(j), :]
            for s in range(1, 6):
                out = out + wm[s] * padded[at(j + s), :]
            result[at(j), :] = out

        loop(rows, meridional)

    gradient = gradient + sum(flux_ref[b] * natural(b, 0) for b in range(bins))
    gbuf[mybin] = gradient
    reducing = []
    for o in range(1, nbin):
        copy = pltpu.make_async_remote_copy(
            src_ref=gbuf.at[mybin],
            dst_ref=gbuf.at[mybin],
            send_sem=gsend_sem.at[o - 1],
            recv_sem=grecv_sem.at[o - 1],
            device_id=(lon, lax.rem(mybin + o, nbin)),
            device_id_type=MESH,
        )
        copy.start()
        reducing.append(copy)
    for b in range(bins):
        for l in range(levels):
            end_ref[b, l] = natural(b, l)
    for step in range(STEPS):
        for copy in copies(step):
            copy.wait_send()
    for o in range(1, nbin):
        source = lax.rem(mybin + nbin - o, nbin)
        pltpu.make_async_remote_copy(
            src_ref=gbuf.at[source],
            dst_ref=gbuf.at[source],
            send_sem=gsend_sem.at[o - 1],
            recv_sem=grecv_sem.at[o - 1],
            device_id=(lon, lax.rem(mybin + o, nbin)),
            device_id_type=MESH,
        ).wait_recv()
    total = gbuf[0]
    for o in range(1, nbin):
        total = total + gbuf[o]
    grad_ref[...] = total
    for copy in reducing:
        copy.wait_send()


def per_device(
    ring,
    nbin,
    adjoint_start,
    base_flux,
    vertical_mixing,
    zonal_fraction,
    meridional_fraction,
    zonal_hops,
    cell_shift,
):
    bins, levels, rows, width = adjoint_start.shape
    bl = bins * levels
    plan = Plan(rows, max(1, rows // 16), ring)
    slots = len(plan.offsets)
    vmem = pl.BlockSpec(memory_space=pltpu.VMEM)
    smem = pl.BlockSpec(memory_space=pltpu.SMEM)
    f32 = jnp.float32
    tile = rows * bl
    return pl.pallas_call(
        functools.partial(kernel, plan, nbin),
        out_shape=(
            jax.ShapeDtypeStruct(adjoint_start.shape, f32),
            jax.ShapeDtypeStruct((rows, width), f32),
        ),
        in_specs=[vmem] * 3 + [smem] * 4,
        out_specs=(vmem, vmem),
        scratch_shapes=[
            pltpu.VMEM((tile, width), jnp.int32),
            pltpu.VMEM((tile, width), jnp.int32),
            pltpu.VMEM((tile, width), f32),
            pltpu.VMEM((tile, width), f32),
            pltpu.VMEM((STEPS, tile, width), f32),
            pltpu.VMEM((STEPS, slots, tile, width), f32),
            pltpu.VMEM((6, tile, width), f32),
            pltpu.VMEM((6, bl, width), f32),
            pltpu.VMEM((tile, width), f32),
            pltpu.VMEM(((rows + 5) * bl, width), f32),
            pltpu.VMEM((tile, width), f32),
            pltpu.VMEM((nbin, rows, width), f32),
            pltpu.SemaphoreType.DMA((STEPS, slots)),
            pltpu.SemaphoreType.DMA((STEPS, slots)),
            pltpu.SemaphoreType.DMA((nbin - 1,)),
            pltpu.SemaphoreType.DMA((nbin - 1,)),
        ],
        compiler_params=pltpu.CompilerParams(
            collective_id=0, has_side_effects=True, vmem_limit_bytes=32 * 1024 * 1024
        ),
    )(
        adjoint_start,
        base_flux,
        vertical_mixing,
        zonal_fraction,
        meridional_fraction,
        zonal_hops,
        cell_shift,
    )


def solution(mesh):
    return jax.shard_map(
        functools.partial(per_device, mesh.shape["lon"], mesh.shape["bin"]),
        mesh=mesh,
        in_specs=(
            P("bin", None, None, "lon"),
            P("bin", None, "lon"),
            P(None, None, "lon"),
            P(),
            P(),
            P(),
            P(),
        ),
        out_specs=(P("bin", None, None, "lon"), P(None, "lon")),
        check_vma=False,
    )
```

time: 83.5 us -> 28.1 us (0.34)
  starting transfers between devices: 44.6 us -> 0 us
  waiting for transfers between devices: 23.9 us -> 0 us
  Pallas kernels: 0 us -> 21.1 us
  blocking collectives: 6.26 us -> 0 us
  other arithmetic: 3.62 us -> 0 us
  local copies, waits for them, and re-layouts: 3.77 us -> 6.01 us
    ppermute x18 -> x0, starting transfers between devices: 44.6 us -> none  [the longest x14 33.8 us: from_behind(): lax.ppermute(value, axis, [(i, (i + by) % length) for i in range(length)])]
    ppermute x18 -> x0, waiting for transfers between devices: 23.9 us -> none  [the longest x14 16.1 us: from_behind(): lax.ppermute(value, axis, [(i, (i + by) % length) for i in range(length)])]
    pallas_call x0 -> x1, Pallas kernels: none -> 21.1 us  [per_device(): pl.pallas_call(functools.partial(kernel, plan, nbin), out_shape=(jax.Shap...]
    psum x1 -> x0, blocking collectives: 6.26 us -> none  [per_device(): gradient_sum = gradient_sum + lax.psum(local_term, 'bin')]
    unnamed x16, local copies, waits for them, and re-layouts: 2.61 us -> 6.01 us
    select_n x18 -> x0, other arithmetic: 1.5 us -> none  [the longest x14 1.2 us: roll_rows(): field_data = jnp.where(chosen, moved, field_data)]
    slice x28 -> x0, local copies, waits for them, and re-layouts: 1.16 us -> none  [the longest x26 1.01 us: roll_rows(): moved = jnp.roll(field_data, -amount, axis=3)]
    add x11 -> x0, other arithmetic: 0.86 us -> none  [the longest x2 0.32 us: zonal_adjoint(): face_flux + weights[offset][:, :, None] * padded[:, :, :, start_col:start...]
  transfers between devices with their start and end apart: 18 -> 0, of which waited for: 11 -> 0; matrix products, arithmetic and copies ran while one was open for 0% -> 0% of each run, Pallas kernels for 0% -> 0%
where the time goes in v1:
time: 28.1 us; the launch traced here: 27.8 us
  Pallas kernels  21.1 us (75%)
  local copies, waits for them, and re-layouts  6.01 us (21%)
  between operations  0.66 us (2%)
    pallas_call x1, Pallas kernels, per_device(): pl.pallas_call(functools.partial(kernel, plan, nbin), out_shape=(jax.Shap...  21.1 us
    unnamed x16, local copies, waits for them, and re-layouts  6.01 us

profile of v1, /device:TPU:0, one launch (start us, length us, event | category | flops | bytes accessed | tf_op | source)
XLA Modules:
  0.0 27.8 jit_solution(15754321212317117918)
XLA Ops:
  0.6 0.0 copy-start
  0.6 0.7 %copy-done = f32[2,4,8,128]{3,2,1,0:T(8,128)S(1)} copy-done((f32[2,4,8,128]{3,2,1,0:T(8,128)S(1)}, f32[2,4,8,128]{3,2,1,0:T(8,128)}, u32[]{:S(2)}) %copy-start) | copy-done | bytes 32792
  1.4 0.0 copy-start.1
  1.4 0.7 %copy-done.1 = f32[3,8,128]{2,1,0:T(8,128)S(1)} copy-done((f32[3,8,128]{2,1,0:T(8,128)S(1)}, f32[3,8,128]{2,1,0:T(8,128)}, u32[]{:S(2)}) %copy-start.1) | copy-done | bytes 12312
  2.1 0.0 copy-start.2
  2.1 0.7 %copy-done.2 = f32[2,8,128]{2,1,0:T(8,128)S(1)} copy-done((f32[2,8,128]{2,1,0:T(8,128)S(1)}, f32[2,8,128]{2,1,0:T(8,128)}, u32[]{:S(2)}) %copy-start.2) | copy-done | bytes 8216
  2.8 0.0 copy-start.3
  2.8 0.7 %copy-done.3 = f32[4,8]{1,0:T(4,128)S(1)} copy-done((f32[4,8]{1,0:T(4,128)S(1)}, f32[4,8]{1,0:T(4,128)}, u32[]{:S(2)}) %copy-start.3) | copy-done | bytes 152
  3.5 0.0 copy-start.4
  3.5 0.7 %copy-done.4 = f32[4]{0:T(128)S(1)} copy-done((f32[4]{0:T(128)S(1)}, f32[4]{0:T(128)}, u32[]{:S(2)}) %copy-start.4) | copy-done | bytes 40
  4.1 0.0 copy-start.5
  4.1 0.7 %copy-done.5 = s32[8]{0:T(128)S(1)} copy-done((s32[8]{0:T(128)S(1)}, s32[8]{0:T(128)}, u32[]{:S(2)}) %copy-start.5) | copy-done | bytes 56
  4.8 0.0 copy-start.6
  4.8 0.7 %copy-done.6 = s32[8]{0:T(128)S(1)} copy-done((s32[8]{0:T(128)S(1)}, s32[8]{0:T(128)}, u32[]{:S(2)}) %copy-start.6) | copy-done | bytes 56
  5.4 21.1 %shard_map.86 = (f32[2,4,8,128]{3,2,1,0:T(8,128)S(1)}, f32[8,128]{1,0:T(8,128)S(1)}) custom-call(f32[2,4,8,128]{3,2,1,0:T(8,128)S(1)} %copy-done, f32[2,8,128]{2,1,0:T(8,128)S(1)} %copy-done.2, f32[3,8,128]{2,1,0:T(8,128)S(1)} %copy-done.1, f32[4,8]{1,0:T(4,128)S(1)} %copy-done.3, f32[4]{0:T(128)S(1)} %copy-done.4, s32[8]{0:T(128)S(1)} %copy-done.5, ...), custom_call_target="tpu_custom_call" | custom-call | tf_op jit(solution)/shard_map/pallas_call | solution.py:355
  26.6 0.6 %copy.11 = f32[2,4,8,128]{3,2,1,0:T(8,128)} copy(f32[2,4,8,128]{3,2,1,0:T(8,128)S(1)} %get-tuple-element.4) | data formatting | bytes 65536
  27.2 0.6 %copy.12 = f32[8,128]{1,0:T(8,128)} copy(f32[8,128]{1,0:T(8,128)S(1)} %get-tuple-element.5) | data formatting | bytes 8192
Async XLA Ops:
  0.6 0.8 %copy-start = (f32[2,4,8,128]{3,2,1,0:T(8,128)S(1)}, f32[2,4,8,128]{3,2,1,0:T(8,128)}, u32[]{:S(2)}) copy-start(f32[2,4,8,128]{3,2,1,0:T(8,128)} %adj_ref.1) | copy-start | bytes 98308
  1.4 0.7 %copy-start.1 = (f32[3,8,128]{2,1,0:T(8,128)S(1)}, f32[3,8,128]{2,1,0:T(8,128)}, u32[]{:S(2)}) copy-start(f32[3,8,128]{2,1,0:T(8,128)} %mix_ref.1) | copy-start | bytes 36868
  2.1 0.7 %copy-start.2 = (f32[2,8,128]{2,1,0:T(8,128)S(1)}, f32[2,8,128]{2,1,0:T(8,128)}, u32[]{:S(2)}) copy-start(f32[2,8,128]{2,1,0:T(8,128)} %flux_ref.1) | copy-start | bytes 24580
  2.8 0.7 %copy-start.3 = (f32[4,8]{1,0:T(4,128)S(1)}, f32[4,8]{1,0:T(4,128)}, u32[]{:S(2)}) copy-start(f32[4,8]{1,0:T(4,128)} %zf_ref.1) | copy-start | bytes 388
  3.5 0.7 %copy-start.4 = (f32[4]{0:T(128)S(1)}, f32[4]{0:T(128)}, u32[]{:S(2)}) copy-start(f32[4]{0:T(128)} %mf_ref.1) | copy-start | bytes 52
  4.1 0.7 %copy-start.5 = (s32[8]{0:T(128)S(1)}, s32[8]{0:T(128)}, u32[]{:S(2)}) copy-start(s32[8]{0:T(128)} %hops_ref.1) | copy-start | bytes 100
  4.8 0.7 %copy-start.6 = (s32[8]{0:T(128)S(1)}, s32[8]{0:T(128)}, u32[]{:S(2)}) copy-start(s32[8]{0:T(128)} %cells_ref.1) | copy-start | bytes 100

commit v2 on v1

--- a/solution.py
+++ b/solution.py
@@ -70,15 +70,23 @@
 def kernel(
     plan,
     nbin,
+    adj_hbm,
+    flux_hbm,
+    mix_hbm,
+    zf_hbm,
+    mf_hbm,
+    hops_hbm,
+    cells_hbm,
+    end_ref,
+    grad_ref,
     adj_ref,
+    mix_ref,
     flux_ref,
-    mix_ref,
     zf_ref,
     mf_ref,
     hops_ref,
     cells_ref,
-    end_ref,
-    grad_ref,
+    load_sem,
     rank,
     shifts_of,
     natural_c,
@@ -101,6 +109,22 @@
     ring = plan.ring
     lon, mybin = lax.axis_index("lon"), lax.axis_index("bin")
 
+    pairs = (
+        (mix_hbm, mix_ref),
+        (adj_hbm, adj_ref),
+        (hops_hbm, hops_ref),
+        (zf_hbm, zf_ref),
+        (cells_hbm, cells_ref),
+        (mf_hbm, mf_ref),
+        (flux_hbm, flux_ref),
+    )
+    loads = [
+        pltpu.make_async_copy(source, target, load_sem.at[i])
+        for i, (source, target) in enumerate(pairs)
+    ]
+    for load in loads:
+        load.start()
+
     barrier = pltpu.get_barrier_semaphore()
     shifts = sorted({t % ring for t in plan.offsets})
     for t in shifts:
@@ -111,6 +135,9 @@
         pl.semaphore_signal(
             barrier, inc=1, device_id=(lon, lax.rem(mybin + nbin - o, nbin)), device_id_type=MESH
         )
+
+    for load in loads[:3]:
+        load.wait()
 
     inverse, ratios, mix = [], [], [mix_ref[l] for l in range(levels - 1)]
     for l in range(levels):
@@ -218,6 +245,8 @@
             copy.start()
 
         if step == 0:
+            for load in loads[3:]:
+                load.wait()
 
             def courant(j):
                 natural_c[at(j), :] = by_level(lambda l: zf_ref[l, j])
@@ -349,7 +378,6 @@
     plan = Plan(rows, max(1, rows // 16), ring)
     slots = len(plan.offsets)
     vmem = pl.BlockSpec(memory_space=pltpu.VMEM)
-    smem = pl.BlockSpec(memory_space=pltpu.SMEM)
     f32 = jnp.float32
     tile = rows * bl
     return pl.pallas_call(
@@ -358,9 +386,17 @@
             jax.ShapeDtypeStruct(adjoint_start.shape, f32),
             jax.ShapeDtypeStruct((rows, width), f32),
         ),
-        in_specs=[vmem] * 3 + [smem] * 4,
+        in_specs=[pl.BlockSpec(memory_space=pltpu.HBM)] * 7,
         out_specs=(vmem, vmem),
         scratch_shapes=[
+            pltpu.VMEM(adjoint_start.shape, f32),
+            pltpu.VMEM(vertical_mixing.shape, f32),
+            pltpu.VMEM(base_flux.shape, f32),
+            pltpu.SMEM(zonal_fraction.shape, f32),
+            pltpu.SMEM(meridional_fraction.shape, f32),
+            pltpu.SMEM(zonal_hops.shape, jnp.int32),
+            pltpu.SMEM(cell_shift.shape, jnp.int32),
+            pltpu.SemaphoreType.DMA((7,)),
             pltpu.VMEM((tile, width), jnp.int32),
             pltpu.VMEM((tile, width), jnp.int32),
             pltpu.VMEM((tile, width), f32),

time: 28.1 us -> 27.6 us (0.982)
  Pallas kernels: 21.1 us -> 20.6 us
    pallas_call x1, Pallas kernels: 21.1 us -> 20.6 us  [per_device(): pl.pallas_call(functools.partial(kernel, plan, nbin), out_shape=(jax.Shap...]
where the time goes in v2:
time: 27.6 us; the launch traced here: 27.3 us
  Pallas kernels  20.6 us (75%)
  local copies, waits for them, and re-layouts  6.01 us (22%)
  between operations  0.66 us (2%)
    pallas_call x1, Pallas kernels, per_device(): pl.pallas_call(functools.partial(kernel, plan, nbin), out_shape=(jax.Shap...  20.6 us
    unnamed x16, local copies, waits for them, and re-layouts  6.01 us

profile of v2, /device:TPU:0, one launch (start us, length us, event | category | flops | bytes accessed | tf_op | source)
XLA Modules:
  0.0 27.3 jit_solution(17401271120034844506)
XLA Ops:
  0.6 0.0 copy-start
  0.6 0.7 %copy-done = f32[2,4,8,128]{3,2,1,0:T(8,128)S(1)} copy-done((f32[2,4,8,128]{3,2,1,0:T(8,128)S(1)}, f32[2,4,8,128]{3,2,1,0:T(8,128)}, u32[]{:S(2)}) %copy-start) | copy-done | bytes 32792
  1.4 0.0 copy-start.1
  1.4 0.7 %copy-done.1 = f32[3,8,128]{2,1,0:T(8,128)S(1)} copy-done((f32[3,8,128]{2,1,0:T(8,128)S(1)}, f32[3,8,128]{2,1,0:T(8,128)}, u32[]{:S(2)}) %copy-start.1) | copy-done | bytes 12312
  2.1 0.0 copy-start.2
  2.1 0.7 %copy-done.2 = f32[2,8,128]{2,1,0:T(8,128)S(1)} copy-done((f32[2,8,128]{2,1,0:T(8,128)S(1)}, f32[2,8,128]{2,1,0:T(8,128)}, u32[]{:S(2)}) %copy-start.2) | copy-done | bytes 8216
  2.8 0.0 copy-start.3
  2.8 0.7 %copy-done.3 = f32[4,8]{1,0:T(4,128)S(1)} copy-done((f32[4,8]{1,0:T(4,128)S(1)}, f32[4,8]{1,0:T(4,128)}, u32[]{:S(2)}) %copy-start.3) | copy-done | bytes 152
  3.5 0.0 copy-start.4
  3.5 0.7 %copy-done.4 = f32[4]{0:T(128)S(1)} copy-done((f32[4]{0:T(128)S(1)}, f32[4]{0:T(128)}, u32[]{:S(2)}) %copy-start.4) | copy-done | bytes 40
  4.1 0.0 copy-start.5
  4.1 0.7 %copy-done.5 = s32[8]{0:T(128)S(1)} copy-done((s32[8]{0:T(128)S(1)}, s32[8]{0:T(128)}, u32[]{:S(2)}) %copy-start.5) | copy-done | bytes 56
  4.8 0.0 copy-start.6
  4.8 0.7 %copy-done.6 = s32[8]{0:T(128)S(1)} copy-done((s32[8]{0:T(128)S(1)}, s32[8]{0:T(128)}, u32[]{:S(2)}) %copy-start.6) | copy-done | bytes 56
  5.4 20.6 %shard_map.86 = (f32[2,4,8,128]{3,2,1,0:T(8,128)S(1)}, f32[8,128]{1,0:T(8,128)S(1)}) custom-call(f32[2,4,8,128]{3,2,1,0:T(8,128)S(1)} %copy-done, f32[2,8,128]{2,1,0:T(8,128)S(1)} %copy-done.2, f32[3,8,128]{2,1,0:T(8,128)S(1)} %copy-done.1, f32[4,8]{1,0:T(4,128)S(1)} %copy-done.3, f32[4]{0:T(128)S(1)} %copy-done.4, s32[8]{0:T(128)S(1)} %copy-done.5, ...), custom_call_target="tpu_custom_call" | custom-call | tf_op jit(solution)/shard_map/pallas_call | solution.py:383
  26.1 0.6 %copy.11 = f32[2,4,8,128]{3,2,1,0:T(8,128)} copy(f32[2,4,8,128]{3,2,1,0:T(8,128)S(1)} %get-tuple-element.4) | data formatting | bytes 65536
  26.7 0.6 %copy.12 = f32[8,128]{1,0:T(8,128)} copy(f32[8,128]{1,0:T(8,128)S(1)} %get-tuple-element.5) | data formatting | bytes 8192
Async XLA Ops:
  0.6 0.8 %copy-start = (f32[2,4,8,128]{3,2,1,0:T(8,128)S(1)}, f32[2,4,8,128]{3,2,1,0:T(8,128)}, u32[]{:S(2)}) copy-start(f32[2,4,8,128]{3,2,1,0:T(8,128)} %adj_hbm.1) | copy-start | bytes 98308
  1.4 0.7 %copy-start.1 = (f32[3,8,128]{2,1,0:T(8,128)S(1)}, f32[3,8,128]{2,1,0:T(8,128)}, u32[]{:S(2)}) copy-start(f32[3,8,128]{2,1,0:T(8,128)} %mix_hbm.1) | copy-start | bytes 36868
  2.1 0.7 %copy-start.2 = (f32[2,8,128]{2,1,0:T(8,128)S(1)}, f32[2,8,128]{2,1,0:T(8,128)}, u32[]{:S(2)}) copy-start(f32[2,8,128]{2,1,0:T(8,128)} %flux_hbm.1) | copy-start | bytes 24580
  2.8 0.7 %copy-start.3 = (f32[4,8]{1,0:T(4,128)S(1)}, f32[4,8]{1,0:T(4,128)}, u32[]{:S(2)}) copy-start(f32[4,8]{1,0:T(4,128)} %zf_hbm.1) | copy-start | bytes 388
  3.5 0.7 %copy-start.4 = (f32[4]{0:T(128)S(1)}, f32[4]{0:T(128)}, u32[]{:S(2)}) copy-start(f32[4]{0:T(128)} %mf_hbm.1) | copy-start | bytes 52
  4.1 0.7 %copy-start.5 = (s32[8]{0:T(128)S(1)}, s32[8]{0:T(128)}, u32[]{:S(2)}) copy-start(s32[8]{0:T(128)} %hops_hbm.1) | copy-start | bytes 100
  4.8 0.7 %copy-start.6 = (s32[8]{0:T(128)S(1)}, s32[8]{0:T(128)}, u32[]{:S(2)}) copy-start(s32[8]{0:T(128)} %cells_hbm.1) | copy-start | bytes 100

commit v3 on v2

--- a/solution.py
+++ b/solution.py
@@ -57,9 +57,22 @@
         for h in range(-HMAX, HMAX + 1):
             self.start[h] = at
             at += count[h]
-        self.offsets = [t for t in range(-HMAX - 2, HMAX + 2) if t % ring]
-        self.offsets.sort(key=lambda t: -abs(t))
-        self.slot = {t: i for i, t in enumerate(self.offsets)}
+        self.rows = rows
+        self.extra = 2 * unit
+        groups = {}
+        for t in range(-HMAX - 2, HMAX + 2):
+            if t % ring:
+                groups.setdefault(t % ring, []).append(t)
+        self.shifts = sorted(groups, key=lambda r: -min(r, ring - r))
+        self.slot = {r: i for i, r in enumerate(self.shifts)}
+        self.part, self.lift = {}, {}
+        for r, both in groups.items():
+            first, count = self.span(both[0])
+            self.lift[both[0]] = 0
+            if len(both) == 2:
+                self.lift[both[1]] = rows
+                count = rows - first + self.span(both[1])[1]
+            self.part[r] = first, count
 
     def span(self, t):
         low, high = max(-t - 2, -HMAX), min(-t + 1, HMAX)
@@ -126,7 +139,7 @@
         load.start()
 
     barrier = pltpu.get_barrier_semaphore()
-    shifts = sorted({t % ring for t in plan.offsets})
+    shifts = plan.shifts
     for t in shifts:
         pl.semaphore_signal(
             barrier, inc=1, device_id=(lax.rem(lon + ring - t, ring), mybin), device_id_type=MESH
@@ -208,17 +221,17 @@
 
     def copies(step):
         found = []
-        for t in plan.offsets:
-            first, count = plan.span(t)
+        for r in plan.shifts:
+            first, count = plan.part[r]
             part = pl.ds(first * bl, count * bl)
-            i = plan.slot[t]
+            i = plan.slot[r]
             found.append(
                 pltpu.make_async_remote_copy(
                     src_ref=sends.at[step, part],
                     dst_ref=recvs.at[step, i, part],
                     send_sem=send_sem.at[step, i],
                     recv_sem=recv_sem.at[step, i],
-                    device_id=(lax.rem(lon + (t % ring), ring), mybin),
+                    device_id=(lax.rem(lon + r, ring), mybin),
                     device_id_type=MESH,
                 )
             )
@@ -237,6 +250,8 @@
         if step == 0:
             loop(rows, find_rank)
         loop(rows, arrange)
+        for p in range(plan.extra):
+            sends[step, at(rows + p), :] = sends[step, at(p), :]
 
         if step == 0:
             pl.semaphore_wait(barrier, len(shifts) + nbin - 1)
@@ -268,10 +283,11 @@
         else:
             gradient = sum(flux_ref[b] * natural(b, 0) for b in range(bins))
 
-        for copy in moving:
-            copy.wait_recv()
-
-        for h in range(-HMAX, HMAX + 1):
+        arrived = set()
+        for h in sorted(range(-HMAX, HMAX + 1), key=abs):
+            for r in sorted({(-h - k) % ring for k in range(-1, 3)} - arrived - {0}):
+                moving[plan.slot[r]].wait_recv()
+                arrived.add(r)
 
             def shift(i):
                 p = plan.start[h] + i
@@ -280,7 +296,7 @@
                     t = -h - k
                     if t % ring == 0:
                         return sends[step, at(p), :]
-                    return recvs[step, plan.slot[t], at(p), :]
+                    return recvs[step, plan.slot[t % ring], at(p + plan.lift[t]), :]
 
                 cells = shifts_of[at(p), :]
                 short = cells < 2
@@ -289,12 +305,10 @@
                 ra = jnp.where(short, t0, t1)
                 rb = jnp.where(short, t1, t2)
                 rc = jnp.where(short, t2, t3)
-                for bit in range((width - 1).bit_length()):
-                    chosen = (first & (1 << bit)) != 0
-                    turn = width - (1 << bit)
-                    ra = jnp.where(chosen, pltpu.roll(ra, turn, 1), ra)
-                    rb = jnp.where(chosen, pltpu.roll(rb, turn, 1), rb)
-                    rc = jnp.where(chosen, pltpu.roll(rc, turn, 1), rc)
+                source = jnp.where(lane < width - first, lane + first, lane + first - width)
+                ra = jnp.take_along_axis(ra, source, axis=1, mode="promise_in_bounds")
+                rb = jnp.take_along_axis(rb, source, axis=1, mode="promise_in_bounds")
+                rc = jnp.take_along_axis(rc, source, axis=1, mode="promise_in_bounds")
                 inside = lane < width - first
                 w0 = jnp.where(inside, ra, rb)
                 w1 = jnp.where(inside, rb, rc)
@@ -376,7 +390,8 @@
     bins, levels, rows, width = adjoint_start.shape
     bl = bins * levels
     plan = Plan(rows, max(1, rows // 16), ring)
-    slots = len(plan.offsets)
+    slots = len(plan.shifts)
+    sent = (rows + plan.extra) * bl
     vmem = pl.BlockSpec(memory_space=pltpu.VMEM)
     f32 = jnp.float32
     tile = rows * bl
@@ -401,8 +416,8 @@
             pltpu.VMEM((tile, width), jnp.int32),
             pltpu.VMEM((tile, width), f32),
             pltpu.VMEM((tile, width), f32),
-            pltpu.VMEM((STEPS, tile, width), f32),
-            pltpu.VMEM((STEPS, slots, tile, width), f32),
+            pltpu.VMEM((STEPS, sent, width), f32),
+            pltpu.VMEM((STEPS, slots, sent, width), f32),
             pltpu.VMEM((6, tile, width), f32),
             pltpu.VMEM((6, bl, width), f32),
             pltpu.VMEM((tile, width), f32),

time: 27.6 us -> 28 us (1.014)
  Pallas kernels: 20.6 us -> 21 us
    pallas_call x1, Pallas kernels: 20.6 us -> 21 us  [per_device(): pl.pallas_call(functools.partial(kernel, plan, nbin), out_shape=(jax.Shap...]
where the time goes in v3:
time: 28 us; the launch traced here: 27.7 us
  Pallas kernels  21 us (75%)
  local copies, waits for them, and re-layouts  6.01 us (21%)
  between operations  0.66 us (2%)
    pallas_call x1, Pallas kernels, per_device(): pl.pallas_call(functools.partial(kernel, plan, nbin), out_shape=(jax.Shap...  21 us
    unnamed x16, local copies, waits for them, and re-layouts  6.01 us

profile of v3, /device:TPU:0, one launch (start us, length us, event | category | flops | bytes accessed | tf_op | source)
XLA Modules:
  0.0 27.7 jit_solution(12800385537820653149)
XLA Ops:
  0.6 0.0 copy-start
  0.6 0.7 %copy-done = f32[2,4,8,128]{3,2,1,0:T(8,128)S(1)} copy-done((f32[2,4,8,128]{3,2,1,0:T(8,128)S(1)}, f32[2,4,8,128]{3,2,1,0:T(8,128)}, u32[]{:S(2)}) %copy-start) | copy-done | bytes 32792
  1.4 0.0 copy-start.1
  1.4 0.7 %copy-done.1 = f32[3,8,128]{2,1,0:T(8,128)S(1)} copy-done((f32[3,8,128]{2,1,0:T(8,128)S(1)}, f32[3,8,128]{2,1,0:T(8,128)}, u32[]{:S(2)}) %copy-start.1) | copy-done | bytes 12312
  2.1 0.0 copy-start.2
  2.1 0.7 %copy-done.2 = f32[2,8,128]{2,1,0:T(8,128)S(1)} copy-done((f32[2,8,128]{2,1,0:T(8,128)S(1)}, f32[2,8,128]{2,1,0:T(8,128)}, u32[]{:S(2)}) %copy-start.2) | copy-done | bytes 8216
  2.8 0.0 copy-start.3
  2.8 0.7 %copy-done.3 = f32[4,8]{1,0:T(4,128)S(1)} copy-done((f32[4,8]{1,0:T(4,128)S(1)}, f32[4,8]{1,0:T(4,128)}, u32[]{:S(2)}) %copy-start.3) | copy-done | bytes 152
  3.5 0.0 copy-start.4
  3.5 0.7 %copy-done.4 = f32[4]{0:T(128)S(1)} copy-done((f32[4]{0:T(128)S(1)}, f32[4]{0:T(128)}, u32[]{:S(2)}) %copy-start.4) | copy-done | bytes 40
  4.1 0.0 copy-start.5
  4.1 0.7 %copy-done.5 = s32[8]{0:T(128)S(1)} copy-done((s32[8]{0:T(128)S(1)}, s32[8]{0:T(128)}, u32[]{:S(2)}) %copy-start.5) | copy-done | bytes 56
  4.8 0.0 copy-start.6
  4.8 0.7 %copy-done.6 = s32[8]{0:T(128)S(1)} copy-done((s32[8]{0:T(128)S(1)}, s32[8]{0:T(128)}, u32[]{:S(2)}) %copy-start.6) | copy-done | bytes 56
  5.4 21.0 %shard_map.86 = (f32[2,4,8,128]{3,2,1,0:T(8,128)S(1)}, f32[8,128]{1,0:T(8,128)S(1)}) custom-call(f32[2,4,8,128]{3,2,1,0:T(8,128)S(1)} %copy-done, f32[2,8,128]{2,1,0:T(8,128)S(1)} %copy-done.2, f32[3,8,128]{2,1,0:T(8,128)S(1)} %copy-done.1, f32[4,8]{1,0:T(4,128)S(1)} %copy-done.3, f32[4]{0:T(128)S(1)} %copy-done.4, s32[8]{0:T(128)S(1)} %copy-done.5, ...), custom_call_target="tpu_custom_call" | custom-call | tf_op jit(solution)/shard_map/pallas_call | solution.py:398
  26.5 0.6 %copy.11 = f32[2,4,8,128]{3,2,1,0:T(8,128)} copy(f32[2,4,8,128]{3,2,1,0:T(8,128)S(1)} %get-tuple-element.4) | data formatting | bytes 65536
  27.1 0.6 %copy.12 = f32[8,128]{1,0:T(8,128)} copy(f32[8,128]{1,0:T(8,128)S(1)} %get-tuple-element.5) | data formatting | bytes 8192
Async XLA Ops:
  0.6 0.8 %copy-start = (f32[2,4,8,128]{3,2,1,0:T(8,128)S(1)}, f32[2,4,8,128]{3,2,1,0:T(8,128)}, u32[]{:S(2)}) copy-start(f32[2,4,8,128]{3,2,1,0:T(8,128)} %adj_hbm.1) | copy-start | bytes 98308
  1.4 0.7 %copy-start.1 = (f32[3,8,128]{2,1,0:T(8,128)S(1)}, f32[3,8,128]{2,1,0:T(8,128)}, u32[]{:S(2)}) copy-start(f32[3,8,128]{2,1,0:T(8,128)} %mix_hbm.1) | copy-start | bytes 36868
  2.1 0.7 %copy-start.2 = (f32[2,8,128]{2,1,0:T(8,128)S(1)}, f32[2,8,128]{2,1,0:T(8,128)}, u32[]{:S(2)}) copy-start(f32[2,8,128]{2,1,0:T(8,128)} %flux_hbm.1) | copy-start | bytes 24580
  2.8 0.7 %copy-start.3 = (f32[4,8]{1,0:T(4,128)S(1)}, f32[4,8]{1,0:T(4,128)}, u32[]{:S(2)}) copy-start(f32[4,8]{1,0:T(4,128)} %zf_hbm.1) | copy-start | bytes 388
  3.5 0.7 %copy-start.4 = (f32[4]{0:T(128)S(1)}, f32[4]{0:T(128)}, u32[]{:S(2)}) copy-start(f32[4]{0:T(128)} %mf_hbm.1) | copy-start | bytes 52
  4.1 0.7 %copy-start.5 = (s32[8]{0:T(128)S(1)}, s32[8]{0:T(128)}, u32[]{:S(2)}) copy-start(s32[8]{0:T(128)} %hops_hbm.1) | copy-start | bytes 100
  4.8 0.7 %copy-start.6 = (s32[8]{0:T(128)S(1)}, s32[8]{0:T(128)}, u32[]{:S(2)}) copy-start(s32[8]{0:T(128)} %cells_hbm.1) | copy-start | bytes 100

commit v4 on v3

--- a/solution.py
+++ b/solution.py
@@ -63,7 +63,7 @@
         for t in range(-HMAX - 2, HMAX + 2):
             if t % ring:
                 groups.setdefault(t % ring, []).append(t)
-        self.shifts = sorted(groups, key=lambda r: -min(r, ring - r))
+        self.shifts = sorted(groups, key=lambda r: min(r, ring - r))
         self.slot = {r: i for i, r in enumerate(self.shifts)}
         self.part, self.lift = {}, {}
         for r, both in groups.items():
@@ -283,11 +283,10 @@
         else:
             gradient = sum(flux_ref[b] * natural(b, 0) for b in range(bins))
 
-        arrived = set()
-        for h in sorted(range(-HMAX, HMAX + 1), key=abs):
-            for r in sorted({(-h - k) % ring for k in range(-1, 3)} - arrived - {0}):
-                moving[plan.slot[r]].wait_recv()
-                arrived.add(r)
+        for copy in moving:
+            copy.wait_recv()
+
+        for h in range(-HMAX, HMAX + 1):
 
             def shift(i):
                 p = plan.start[h] + i

time: 28 us -> 25.4 us (0.907)
  Pallas kernels: 21 us -> 18.4 us
    pallas_call x1, Pallas kernels: 21 us -> 18.4 us  [per_device(): pl.pallas_call(functools.partial(kernel, plan, nbin), out_shape=(jax.Shap...]
where the time goes in v4:
time: 25.4 us; the launch traced here: 25 us
  Pallas kernels  18.4 us (72%)
  local copies, waits for them, and re-layouts  6.01 us (24%)
  between operations  0.66 us (3%)
    pallas_call x1, Pallas kernels, per_device(): pl.pallas_call(functools.partial(kernel, plan, nbin), out_shape=(jax.Shap...  18.4 us
    unnamed x16, local copies, waits for them, and re-layouts  6.01 us

profile of v4, /device:TPU:0, one launch (start us, length us, event | category | flops | bytes accessed | tf_op | source)
XLA Modules:
  0.0 25.0 jit_solution(8626900369882227553)
XLA Ops:
  0.6 0.0 copy-start
  0.6 0.7 %copy-done = f32[2,4,8,128]{3,2,1,0:T(8,128)S(1)} copy-done((f32[2,4,8,128]{3,2,1,0:T(8,128)S(1)}, f32[2,4,8,128]{3,2,1,0:T(8,128)}, u32[]{:S(2)}) %copy-start) | copy-done | bytes 32792
  1.4 0.0 copy-start.1
  1.4 0.7 %copy-done.1 = f32[3,8,128]{2,1,0:T(8,128)S(1)} copy-done((f32[3,8,128]{2,1,0:T(8,128)S(1)}, f32[3,8,128]{2,1,0:T(8,128)}, u32[]{:S(2)}) %copy-start.1) | copy-done | bytes 12312
  2.1 0.0 copy-start.2
  2.1 0.7 %copy-done.2 = f32[2,8,128]{2,1,0:T(8,128)S(1)} copy-done((f32[2,8,128]{2,1,0:T(8,128)S(1)}, f32[2,8,128]{2,1,0:T(8,128)}, u32[]{:S(2)}) %copy-start.2) | copy-done | bytes 8216
  2.8 0.0 copy-start.3
  2.8 0.7 %copy-done.3 = f32[4,8]{1,0:T(4,128)S(1)} copy-done((f32[4,8]{1,0:T(4,128)S(1)}, f32[4,8]{1,0:T(4,128)}, u32[]{:S(2)}) %copy-start.3) | copy-done | bytes 152
  3.5 0.0 copy-start.4
  3.5 0.7 %copy-done.4 = f32[4]{0:T(128)S(1)} copy-done((f32[4]{0:T(128)S(1)}, f32[4]{0:T(128)}, u32[]{:S(2)}) %copy-start.4) | copy-done | bytes 40
  4.1 0.0 copy-start.5
  4.1 0.7 %copy-done.5 = s32[8]{0:T(128)S(1)} copy-done((s32[8]{0:T(128)S(1)}, s32[8]{0:T(128)}, u32[]{:S(2)}) %copy-start.5) | copy-done | bytes 56
  4.8 0.0 copy-start.6
  4.8 0.7 %copy-done.6 = s32[8]{0:T(128)S(1)} copy-done((s32[8]{0:T(128)S(1)}, s32[8]{0:T(128)}, u32[]{:S(2)}) %copy-start.6) | copy-done | bytes 56
  5.4 18.4 %shard_map.86 = (f32[2,4,8,128]{3,2,1,0:T(8,128)S(1)}, f32[8,128]{1,0:T(8,128)S(1)}) custom-call(f32[2,4,8,128]{3,2,1,0:T(8,128)S(1)} %copy-done, f32[2,8,128]{2,1,0:T(8,128)S(1)} %copy-done.2, f32[3,8,128]{2,1,0:T(8,128)S(1)} %copy-done.1, f32[4,8]{1,0:T(4,128)S(1)} %copy-done.3, f32[4]{0:T(128)S(1)} %copy-done.4, s32[8]{0:T(128)S(1)} %copy-done.5, ...), custom_call_target="tpu_custom_call" | custom-call | tf_op jit(solution)/shard_map/pallas_call | solution.py:397
  23.8 0.6 %copy.11 = f32[2,4,8,128]{3,2,1,0:T(8,128)} copy(f32[2,4,8,128]{3,2,1,0:T(8,128)S(1)} %get-tuple-element.4) | data formatting | bytes 65536
  24.4 0.6 %copy.12 = f32[8,128]{1,0:T(8,128)} copy(f32[8,128]{1,0:T(8,128)S(1)} %get-tuple-element.5) | data formatting | bytes 8192
Async XLA Ops:
  0.6 0.8 %copy-start = (f32[2,4,8,128]{3,2,1,0:T(8,128)S(1)}, f32[2,4,8,128]{3,2,1,0:T(8,128)}, u32[]{:S(2)}) copy-start(f32[2,4,8,128]{3,2,1,0:T(8,128)} %adj_hbm.1) | copy-start | bytes 98308
  1.4 0.7 %copy-start.1 = (f32[3,8,128]{2,1,0:T(8,128)S(1)}, f32[3,8,128]{2,1,0:T(8,128)}, u32[]{:S(2)}) copy-start(f32[3,8,128]{2,1,0:T(8,128)} %mix_hbm.1) | copy-start | bytes 36868
  2.1 0.7 %copy-start.2 = (f32[2,8,128]{2,1,0:T(8,128)S(1)}, f32[2,8,128]{2,1,0:T(8,128)}, u32[]{:S(2)}) copy-start(f32[2,8,128]{2,1,0:T(8,128)} %flux_hbm.1) | copy-start | bytes 24580
  2.8 0.7 %copy-start.3 = (f32[4,8]{1,0:T(4,128)S(1)}, f32[4,8]{1,0:T(4,128)}, u32[]{:S(2)}) copy-start(f32[4,8]{1,0:T(4,128)} %zf_hbm.1) | copy-start | bytes 388
  3.5 0.7 %copy-start.4 = (f32[4]{0:T(128)S(1)}, f32[4]{0:T(128)}, u32[]{:S(2)}) copy-start(f32[4]{0:T(128)} %mf_hbm.1) | copy-start | bytes 52
  4.1 0.7 %copy-start.5 = (s32[8]{0:T(128)S(1)}, s32[8]{0:T(128)}, u32[]{:S(2)}) copy-start(s32[8]{0:T(128)} %hops_hbm.1) | copy-start | bytes 100
  4.8 0.7 %copy-start.6 = (s32[8]{0:T(128)S(1)}, s32[8]{0:T(128)}, u32[]{:S(2)}) copy-start(s32[8]{0:T(128)} %cells_hbm.1) | copy-start | bytes 100

commit v5 on v4

--- a/solution.py
+++ b/solution.py
@@ -122,6 +122,17 @@
     ring = plan.ring
     lon, mybin = lax.axis_index("lon"), lax.axis_index("bin")
 
+    barrier = pltpu.get_barrier_semaphore()
+    shifts = plan.shifts
+    for t in shifts:
+        pl.semaphore_signal(
+            barrier, inc=1, device_id=(lax.rem(lon + ring - t, ring), mybin), device_id_type=MESH
+        )
+    for o in range(1, nbin):
+        pl.semaphore_signal(
+            barrier, inc=1, device_id=(lon, lax.rem(mybin + nbin - o, nbin)), device_id_type=MESH
+        )
+
     pairs = (
         (mix_hbm, mix_ref),
         (adj_hbm, adj_ref),
@@ -137,17 +148,6 @@
     ]
     for load in loads:
         load.start()
-
-    barrier = pltpu.get_barrier_semaphore()
-    shifts = plan.shifts
-    for t in shifts:
-        pl.semaphore_signal(
-            barrier, inc=1, device_id=(lax.rem(lon + ring - t, ring), mybin), device_id_type=MESH
-        )
-    for o in range(1, nbin):
-        pl.semaphore_signal(
-            barrier, inc=1, device_id=(lon, lax.rem(mybin + nbin - o, nbin)), device_id_type=MESH
-        )
 
     for load in loads[:3]:
         load.wait()
@@ -254,12 +254,6 @@
             sends[step, at(rows + p), :] = sends[step, at(p), :]
 
         if step == 0:
-            pl.semaphore_wait(barrier, len(shifts) + nbin - 1)
-        moving = copies(step)
-        for copy in moving:
-            copy.start()
-
-        if step == 0:
             for load in loads[3:]:
                 load.wait()
 
@@ -280,7 +274,12 @@
             nothing = jnp.zeros((bl, width), jnp.float32)
             for row in (0, 1, rows + 2, rows + 3, rows + 4):
                 padded[at(row), :] = nothing
-        else:
+            pl.semaphore_wait(barrier, len(shifts) + nbin - 1)
+        moving = copies(step)
+        for copy in moving:
+            copy.start()
+
+        if step:
             gradient = sum(flux_ref[b] * natural(b, 0) for b in range(bins))
 
         for copy in moving:

time: 25.4 us -> 25.3 us (level)
  no operation moved by 1% of the time
where the time goes in v5:
time: 25.3 us; the launch traced here: 25 us
  Pallas kernels  18.3 us (72%)
  local copies, waits for them, and re-layouts  6.01 us (24%)
  between operations  0.66 us (3%)
    pallas_call x1, Pallas kernels, per_device(): pl.pallas_call(functools.partial(kernel, plan, nbin), out_shape=(jax.Shap...  18.3 us
    unnamed x16, local copies, waits for them, and re-layouts  6.01 us

profile of v5, /device:TPU:0, one launch (start us, length us, event | category | flops | bytes accessed | tf_op | source)
XLA Modules:
  0.0 25.0 jit_solution(609244358633598033)
XLA Ops:
  0.6 0.0 copy-start
  0.6 0.7 %copy-done = f32[2,4,8,128]{3,2,1,0:T(8,128)S(1)} copy-done((f32[2,4,8,128]{3,2,1,0:T(8,128)S(1)}, f32[2,4,8,128]{3,2,1,0:T(8,128)}, u32[]{:S(2)}) %copy-start) | copy-done | bytes 32792
  1.4 0.0 copy-start.1
  1.4 0.7 %copy-done.1 = f32[3,8,128]{2,1,0:T(8,128)S(1)} copy-done((f32[3,8,128]{2,1,0:T(8,128)S(1)}, f32[3,8,128]{2,1,0:T(8,128)}, u32[]{:S(2)}) %copy-start.1) | copy-done | bytes 12312
  2.1 0.0 copy-start.2
  2.1 0.7 %copy-done.2 = f32[2,8,128]{2,1,0:T(8,128)S(1)} copy-done((f32[2,8,128]{2,1,0:T(8,128)S(1)}, f32[2,8,128]{2,1,0:T(8,128)}, u32[]{:S(2)}) %copy-start.2) | copy-done | bytes 8216
  2.8 0.0 copy-start.3
  2.8 0.7 %copy-done.3 = f32[4,8]{1,0:T(4,128)S(1)} copy-done((f32[4,8]{1,0:T(4,128)S(1)}, f32[4,8]{1,0:T(4,128)}, u32[]{:S(2)}) %copy-start.3) | copy-done | bytes 152
  3.5 0.0 copy-start.4
  3.5 0.7 %copy-done.4 = f32[4]{0:T(128)S(1)} copy-done((f32[4]{0:T(128)S(1)}, f32[4]{0:T(128)}, u32[]{:S(2)}) %copy-start.4) | copy-done | bytes 40
  4.1 0.0 copy-start.5
  4.1 0.7 %copy-done.5 = s32[8]{0:T(128)S(1)} copy-done((s32[8]{0:T(128)S(1)}, s32[8]{0:T(128)}, u32[]{:S(2)}) %copy-start.5) | copy-done | bytes 56
  4.8 0.0 copy-start.6
  4.8 0.7 %copy-done.6 = s32[8]{0:T(128)S(1)} copy-done((s32[8]{0:T(128)S(1)}, s32[8]{0:T(128)}, u32[]{:S(2)}) %copy-start.6) | copy-done | bytes 56
  5.4 18.3 %shard_map.86 = (f32[2,4,8,128]{3,2,1,0:T(8,128)S(1)}, f32[8,128]{1,0:T(8,128)S(1)}) custom-call(f32[2,4,8,128]{3,2,1,0:T(8,128)S(1)} %copy-done, f32[2,8,128]{2,1,0:T(8,128)S(1)} %copy-done.2, f32[3,8,128]{2,1,0:T(8,128)S(1)} %copy-done.1, f32[4,8]{1,0:T(4,128)S(1)} %copy-done.3, f32[4]{0:T(128)S(1)} %copy-done.4, s32[8]{0:T(128)S(1)} %copy-done.5, ...), custom_call_target="tpu_custom_call" | custom-call | tf_op jit(solution)/shard_map/pallas_call | solution.py:396
  23.8 0.6 %copy.11 = f32[2,4,8,128]{3,2,1,0:T(8,128)} copy(f32[2,4,8,128]{3,2,1,0:T(8,128)S(1)} %get-tuple-element.4) | data formatting | bytes 65536
  24.4 0.6 %copy.12 = f32[8,128]{1,0:T(8,128)} copy(f32[8,128]{1,0:T(8,128)S(1)} %get-tuple-element.5) | data formatting | bytes 8192
Async XLA Ops:
  0.6 0.8 %copy-start = (f32[2,4,8,128]{3,2,1,0:T(8,128)S(1)}, f32[2,4,8,128]{3,2,1,0:T(8,128)}, u32[]{:S(2)}) copy-start(f32[2,4,8,128]{3,2,1,0:T(8,128)} %adj_hbm.1) | copy-start | bytes 98308
  1.4 0.7 %copy-start.1 = (f32[3,8,128]{2,1,0:T(8,128)S(1)}, f32[3,8,128]{2,1,0:T(8,128)}, u32[]{:S(2)}) copy-start(f32[3,8,128]{2,1,0:T(8,128)} %mix_hbm.1) | copy-start | bytes 36868
  2.1 0.7 %copy-start.2 = (f32[2,8,128]{2,1,0:T(8,128)S(1)}, f32[2,8,128]{2,1,0:T(8,128)}, u32[]{:S(2)}) copy-start(f32[2,8,128]{2,1,0:T(8,128)} %flux_hbm.1) | copy-start | bytes 24580
  2.8 0.7 %copy-start.3 = (f32[4,8]{1,0:T(4,128)S(1)}, f32[4,8]{1,0:T(4,128)}, u32[]{:S(2)}) copy-start(f32[4,8]{1,0:T(4,128)} %zf_hbm.1) | copy-start | bytes 388
  3.5 0.7 %copy-start.4 = (f32[4]{0:T(128)S(1)}, f32[4]{0:T(128)}, u32[]{:S(2)}) copy-start(f32[4]{0:T(128)} %mf_hbm.1) | copy-start | bytes 52
  4.1 0.7 %copy-start.5 = (s32[8]{0:T(128)S(1)}, s32[8]{0:T(128)}, u32[]{:S(2)}) copy-start(s32[8]{0:T(128)} %hops_hbm.1) | copy-start | bytes 100
  4.8 0.7 %copy-start.6 = (s32[8]{0:T(128)S(1)}, s32[8]{0:T(128)}, u32[]{:S(2)}) copy-start(s32[8]{0:T(128)} %cells_hbm.1) | copy-start | bytes 100
